TPU v7x, 32 devices: a whole 2x2x4 slice. The times are simulated.
32 devices in a mesh: seq: 8 (over z, y), dp: 4 (over x, core).
Axes of the slice: x: 2, y: 2, z: 4, core: 2. Of those that a mesh axis runs over, the one named last changes fastest.
Arguments:
- inputs: bfloat16 [4, 2048, 512], P('dp', 'seq'), may hold values from -6 to 6
- write_vecs: bfloat16 [4, 2048, 128], P('dp', 'seq'), may hold values from -6 to 6
- read_vecs: bfloat16 [4, 2048, 128], P('dp', 'seq'), may hold values from -0.5 to 0.5
- dt_code: int32 [4, 8, 2048], P('dp', None, 'seq'), may hold values from 1 to 10240
- a_rate: float32 [8], replicated, may hold values from 0.4 to 85.333333
- w_out: bfloat16 [512, 2560], replicated, may hold values from -0.125 to 0.125
- grad_out: bfloat16 [4, 2048, 2560], P('dp', 'seq'), may hold values from -0.59765625 to 0.59765625
Outputs:
- outputs: bfloat16 [4, 2048, 512], P('dp', 'seq')
- grad_inputs: bfloat16 [4, 2048, 512], P('dp', 'seq')
- grad_write: bfloat16 [4, 2048, 128], P('dp', 'seq')
- grad_read: bfloat16 [4, 2048, 128], P('dp', 'seq')
- grad_w_out: float32 [512, 2560], P('seq')
All inputs are finite; a program needn't handle non-finite values.
Results may differ from a plain program's by a relative error of at most 0.0055.
Values sent between devices are 32-bit elements; how exact they have to be, the bound alone decides.
A program may use at most 128 MiB of HBM per device.

v0:
```python
import functools

import jax
import jax.numpy as jnp
from jax import lax
from jax.experimental import pallas as pl
from jax.experimental.pallas import tpu as pltpu
from jax.sharding import PartitionSpec as P

HEAD_DIM = 64
STATE = 128
HEADS = 8
HALF = 256
ALONE = 384
PIECES = ((True, 0, 256), (True, 256, 256), (False, 0, 256), (False, 256, 128))
VMEM_BYTES = 60 * 1024 * 1024
CHANNELS = HEADS * HEAD_DIM
MESH = pl.DeviceIdType.MESH
f32 = jnp.float32
bf16 = jnp.bfloat16


def dot(a, b, dims=((1,), (0,))):
    return lax.dot_general(a, b, (dims, ((), ())), preferred_element_type=f32)


NT = ((1,), (1,))
TN = ((0,), (0,))


def widen(cols):
    rows = cols.shape[0]
    return jnp.concatenate(
        [jnp.broadcast_to(cols[:, h : h + 1], (rows, HEAD_DIM)) for h in range(HEADS)], axis=1
    )


def one_minus_exp(w):
    series = 1.0 - w * (1.0 / 9.0)
    for k in (8, 7, 6, 5, 4, 3, 2):
        series = 1.0 - w * (1.0 / k) * series
    return jnp.where(w < 0.5, w * series, 1.0 - jnp.exp(-w))


def kernel(
    n, m, seq_len,
    x_hbm, b_hbm, c_hbm, dt_hbm, arow_ref, w_hbm, g_hbm,
    out_hbm, gin_hbm, gwrite_hbm, gread_hbm, gw_hbm,
    x_ref, b_ref, c_ref, dt_ref, w_ref, g_ref,
    out_ref, gin_ref, gwrite_ref, gread_ref, gw_ref,
    gsend, gall, gpsend, gprecv, fsend, frecv, fback, fin, asend, arecv, aback, ain, oall,
    part0, part1, part2, part3, ybuf0, ybuf1, ybuf2, ybuf3, rsbuf0, rsbuf1, rsbuf2, rsbuf3,
    tsend, trecv, both0, both1, gwall2, gwall3,
    g_ss, g_rs, gp_ss, gp_rs, f_ss, f_rs, a_ss, a_rs, fb_ss, fb_rs, ab_ss, ab_rs,
    o_ss, o_rs, y_ss, y_rs, r_ss, r_rs, t_ss, t_rs, b_ss, b_rs, w_ss, w_rs, in_sem, out_sem,
):
    parts, ybufs = (part0, part1, part2, part3), (ybuf0, ybuf1, ybuf2, ybuf3)
    rsbufs = (rsbuf0, rsbuf1, rsbuf2, rsbuf3)
    boths, gwalls = (both0, both1), (None, None, gwall2, gwall3)
    me = lax.axis_index("seq")
    dp = lax.axis_index("dp")
    tokens = x_ref.shape[1]
    pairs = n // 2
    z, y = me // 2, lax.rem(me, 2)
    loads = [
        pltpu.make_async_copy(src, dst, in_sem.at[i])
        for i, (src, dst) in enumerate(
            [(dt_hbm, dt_ref), (x_hbm, x_ref), (b_hbm, b_ref), (c_hbm, c_ref), (g_hbm, g_ref), (w_hbm, w_ref)]
        )
    ]
    for load in loads:
        load.start()
    stores = [
        pltpu.make_async_copy(src, dst, out_sem.at[i])
        for i, (src, dst) in enumerate(
            [(out_ref, out_hbm), (gin_ref, gin_hbm), (gwrite_ref, gwrite_hbm), (gread_ref, gread_hbm), (gw_ref, gw_hbm)]
        )
    ]
    rows = CHANNELS // n
    per_head = HEAD_DIM // rows
    cols = gsend.shape[2]
    wide = gprecv.shape[1]
    base = 2 * wide
    side = lax.rem(dp, 2)

    def seq_copy(src, dst, ss, rs, k, wait):
        to = lax.rem(me + k, n)
        source = lax.rem(me + n - k, n)
        return pltpu.make_async_remote_copy(
            src_ref=src.at[to],
            dst_ref=dst.at[source] if wait else dst.at[me],
            send_sem=ss.at[k],
            recv_sem=rs.at[k],
            device_id={"seq": to},
            device_id_type=MESH,
        )

    def seq_start(src, dst, ss, rs):
        def body(k, carry):
            seq_copy(src, dst, ss, rs, k, False).start()
            return carry

        lax.fori_loop(1, n, body, 0)

    def seq_wait(src, dst, ss, rs):
        def body(k, carry):
            seq_copy(src, dst, ss, rs, k, True).wait()
            return carry

        lax.fori_loop(1, n, body, 0)

    def dp_copy(src, dst, ss, rs, k, wait):
        to = lax.rem(dp + k, m)
        source = lax.rem(dp + m - k, m)
        return pltpu.make_async_remote_copy(
            src_ref=src.at[to],
            dst_ref=dst.at[source] if wait else dst.at[dp],
            send_sem=ss.at[k],
            recv_sem=rs.at[k],
            device_id={"dp": to},
            device_id_type=MESH,
        )

    bits = [1 << i for i in reversed(range(m.bit_length() - 1))]

    def dp_send(buf, ss, rs, off, bit):
        slot = jnp.bitwise_xor(dp, off)
        return pltpu.make_async_remote_copy(
            src_ref=buf.at[slot],
            dst_ref=buf.at[slot],
            send_sem=ss.at[off + bit],
            recv_sem=rs.at[off + bit],
            device_id={"dp": jnp.bitwise_xor(dp, bit)},
            device_id_type=MESH,
        )

    def dp_arrived(buf, ss, rs, off):
        slot = jnp.bitwise_xor(dp, off)
        bit = off & -off
        pltpu.make_async_remote_copy(
            src_ref=buf.at[slot],
            dst_ref=buf.at[slot],
            send_sem=ss.at[off],
            recv_sem=rs.at[off],
            device_id={"dp": jnp.bitwise_xor(dp, bit)},
            device_id_type=MESH,
        ).wait_recv()

    def dp_own(buf, ss, rs):
        for bit in bits:
            dp_send(buf, ss, rs, 0, bit).start()

    def dp_rest(buf, ss, rs, here=()):
        here = set(here)
        for bit in bits:
            for off in range(2 * bit, m, 2 * bit):
                if off not in here:
                    dp_arrived(buf, ss, rs, off)
                    here.add(off)
                dp_send(buf, ss, rs, off, bit).start()
        for off in range(1, m):
            if off not in here:
                dp_arrived(buf, ss, rs, off)

    def dp_sent(buf, ss, rs):
        for bit in bits:
            for off in range(0, m, 2 * bit):
                dp_send(buf, ss, rs, off, bit).wait_send()

    barrier = pltpu.get_barrier_semaphore()

    def greet_seq(k, carry):
        pl.semaphore_signal(
            barrier, inc=1, device_id={"seq": lax.rem(me + k, n)}, device_id_type=MESH
        )
        return carry

    def greet_dp(k, carry):
        pl.semaphore_signal(
            barrier, inc=1, device_id={"dp": lax.rem(dp + k, m)}, device_id_type=MESH
        )
        return carry

    lax.fori_loop(1, n, greet_seq, 0)
    lax.fori_loop(1, m, greet_dp, 0)

    loads[0].wait()
    dt = dt_ref[0]
    at_row = lax.broadcasted_iota(jnp.int32, (tokens, tokens), 0)
    at_col = lax.broadcasted_iota(jnp.int32, (tokens, tokens), 1)
    lower = at_row >= at_col
    low_mat = lower.astype(f32).astype(bf16)
    eye = (at_row == at_col).astype(f32).astype(bf16)
    digits = [
        part_of.astype(f32).astype(bf16) for part_of in (dt & 127, (dt >> 7) & 127, dt >> 14)
    ]

    def joined(pieces):
        whole = [p.astype(jnp.int32) for p in pieces]
        return whole[0] + whole[1] * 128 + whole[2] * 16384

    cum_row = joined([dot(d, low_mat, NT) for d in digits])
    cum_col = joined([dot(low_mat, d, NT) for d in digits])
    dt_col = joined([dot(eye, d, NT) for d in digits])
    rate_row = arow_ref[...] * (1.0 / (8.0 * seq_len))
    same = lax.broadcasted_iota(jnp.int32, (HEADS, HEADS), 0) == lax.broadcasted_iota(
        jnp.int32, (HEADS, HEADS), 1
    )
    rate_col = jnp.sum(jnp.where(same, rate_row, 0.0), axis=1, keepdims=True)
    weight = jnp.sqrt(one_minus_exp(2.0 * (rate_row * dt_col.astype(f32))))
    head = jnp.exp(-(rate_row * cum_col.astype(f32)))
    tail = jnp.exp(-(rate_row * (cum_col[tokens - 1 :, :] - cum_col).astype(f32)))
    totals = jnp.broadcast_to(
        jnp.exp(-(rate_col * cum_row[:, tokens - 1 :].astype(f32))), (HEADS, STATE)
    )
    weight_w, head_w, tail_w = widen(weight), widen(head), widen(tail)

    for load in loads[1:4]:
        load.wait()
    b = b_ref[0]
    c = c_ref[0]
    weighted = x_ref[0].astype(f32) * weight_w
    tailed = (weighted * tail_w).astype(bf16)
    weighted = weighted.astype(bf16)
    own = dot(tailed, b, TN)
    fsend[:, :rows, :] = own.reshape(n, rows, STATE)
    fsend[:, rows:, :] = jnp.broadcast_to(totals[None], (n, HEADS, STATE))

    pl.semaphore_wait(barrier, n - 1 + m - 1)
    seq_start(fsend, frecv, f_ss, f_rs)

    loads[4].wait()
    grad = g_ref[0]
    for d in range(m):
        gsend[d] = grad[:, base + d * cols : base + (d + 1) * cols].astype(f32)
    low_cols, high_cols = grad[:, :wide].astype(f32), grad[:, wide:base].astype(f32)
    gpsend[...] = jnp.where(side == 0, high_cols, low_cols)
    gp_own = jnp.where(side == 0, low_cols, high_cols).astype(bf16)

    def pair_copy(src, dst, ss, rs):
        return pltpu.make_async_remote_copy(
            src_ref=src,
            dst_ref=dst,
            send_sem=ss,
            recv_sem=rs,
            device_id={"dp": jnp.bitwise_xor(dp, 1)},
            device_id_type=MESH,
        )

    gp_copy = pair_copy(gpsend, gprecv, gp_ss.at[0], gp_rs.at[0])

    def g_start(k, carry):
        dp_copy(gsend, gall, g_ss, g_rs, k, False).start()
        return carry

    def g_wait(k, carry):
        dp_copy(gsend, gall, g_ss, g_rs, k, True).wait()
        return carry

    lax.fori_loop(1, m, g_start, 0)
    gp_copy.start()
    gall[dp] = gsend[dp]

    loads[5].wait()
    grad_y = dot(grad, w_ref[...], NT).astype(bf16)
    grad_dec = (grad_y.astype(f32) * head_w).astype(bf16)
    own_adj = dot(grad_dec, c, TN)
    asend[:, :rows, :] = own_adj.reshape(n, rows, STATE)
    asend[:, rows:, :] = jnp.broadcast_to(totals[None], (n, HEADS, STATE))
    seq_start(asend, arecv, a_ss, a_rs)

    my_head = (me * rows) // HEAD_DIM
    frecv[me] = fsend[me]
    arecv[me] = asend[me]

    def scan_rows(buf, back, reverse):
        def body(step, state):
            s = n - 1 - step if reverse else step
            back[s] = state
            decay = buf[s, pl.ds(rows + my_head, 1), :]
            return decay * state + buf[s, :rows, :]

        lax.fori_loop(0, n, body, jnp.zeros((rows, STATE), f32))

    seq_wait(fsend, frecv, f_ss, f_rs)
    scan_rows(frecv, fback, False)
    seq_start(fback, fin, fb_ss, fb_rs)
    fin[me] = fback[me]

    scores = dot(c, b, NT)
    y_parts, gx_parts = [], []

    def within(heads, pair):
        for h in heads:
            span = slice(h * HEAD_DIM, (h + 1) * HEAD_DIM)
            gap = (cum_col[:, h : h + 1] - cum_row[h : h + 1, :]).astype(f32)
            mask = jnp.exp(jnp.where(lower, -(rate_row[:, h : h + 1] * gap), -jnp.inf))
            mixed = (mask * scores).astype(bf16)
            w_h, g_h = weighted[:, span], grad_y[:, span]
            y_parts.append(dot(mixed, w_h))
            gx_parts.append(dot(mixed, g_h, TN))
            pair = pair + mask * dot(g_h, w_h, NT)
        return pair

    pair = within(range(HEADS // 2), jnp.zeros((tokens, tokens), f32))
    seq_wait(asend, arecv, a_ss, a_rs)
    scan_rows(arecv, aback, True)
    seq_start(aback, ain, ab_ss, ab_rs)
    ain[me] = aback[me]
    pair = within(range(HEADS // 2, HEADS), pair)
    y_intra = jnp.concatenate(y_parts, axis=1)
    gx_intra = jnp.concatenate(gx_parts, axis=1)
    pair = pair.astype(bf16)
    read_intra = dot(pair, b)
    write_intra = dot(pair, c, TN)

    seq_wait(fback, fin, fb_ss, fb_rs)
    state_in = fin[...].reshape(CHANNELS, STATE).astype(bf16)
    out = (y_intra + dot(c, state_in, NT) * head_w).astype(bf16)
    halves = CHANNELS // HALF
    for j in range(halves):
        oall[j, dp] = out[:, j * HALF : (j + 1) * HALF].astype(f32)
        dp_own(oall.at[j], o_ss.at[j], o_rs.at[j])
    out_ref[0] = out
    stores[0].start()

    def to_partner(i):
        return pltpu.make_async_remote_copy(
            src_ref=parts[i].at[1 - y],
            dst_ref=ybufs[i],
            send_sem=y_ss.at[i],
            recv_sem=y_rs.at[i],
            device_id={"seq": 2 * z + 1 - y},
            device_id_type=MESH,
        )

    def to_owner(i, p, source):
        return pltpu.make_async_remote_copy(
            src_ref=parts[i].at[y, p],
            dst_ref=rsbufs[i].at[source],
            send_sem=r_ss.at[i, p],
            recv_sem=r_rs.at[i, source],
            device_id={"seq": 2 * p + y},
            device_id_type=MESH,
        )

    def send_part(i, total):
        split = total.reshape(pairs, 2, rows, total.shape[1])
        parts[i][0] = split[:, 0]
        parts[i][1] = split[:, 1]
        to_partner(i).start()

    def join(i):
        to_partner(i).wait_recv()
        parts[i][y] = parts[i][y] + ybufs[i][...]

        def body(k, carry):
            to_owner(i, lax.rem(z + k, pairs), z).start()
            return carry

        lax.fori_loop(1, pairs, body, 0)

    def owned(i):
        def body(k, acc):
            source = lax.rem(z + k, pairs)
            to_owner(i, source, source).wait()
            return acc + rsbufs[i][source]

        return lax.fori_loop(1, pairs, body, parts[i][y, z])

    gp_copy.wait()
    gp_got = gprecv[...].astype(bf16)
    mate = jnp.bitwise_xor(dp, 1)
    for j in range(halves):
        dp_arrived(oall.at[j], o_ss.at[j], o_rs.at[j], 1)
    mate_out = [oall[j, mate].astype(bf16) for j in range(halves)]
    for i, (paired, start, size) in enumerate(PIECES):
        if paired:
            at = slice(start, start + size)
            own_sum = dot(out, gp_own[:, at], TN)
            mate_sum = jnp.concatenate([dot(o, gp_got[:, at], TN) for o in mate_out], axis=0)
            send_part(i, own_sum + mate_sum)
    gread_ref[0] = (read_intra + dot(grad_dec, state_in)).astype(bf16)
    stores[3].start()
    lax.fori_loop(1, m, g_wait, 0)
    gall_half = [gall[d].astype(bf16) for d in range(m)]
    for i in range(2):
        join(i)
        dp_rest(oall.at[i], o_ss.at[i], o_rs.at[i], (1,))

    for i, (paired, start, size) in enumerate(PIECES):
        if not paired:
            at = slice(start, start + size)
            blocks = []
            for j in range(halves):
                total = jnp.zeros((HALF, size), f32)
                for d in range(m):
                    total = total + dot(oall[j, d].astype(bf16), gall_half[d][:, at], TN)
                blocks.append(total)
            send_part(i, jnp.concatenate(blocks, axis=0))

    def across(i, at):
        return pltpu.make_async_remote_copy(
            src_ref=tsend.at[i, at],
            dst_ref=trecv.at[i, at],
            send_sem=t_ss.at[i, at],
            recv_sem=t_rs.at[i, at],
            device_id={"dp": jnp.bitwise_xor(dp, bits[at])},
            device_id_type=MESH,
        )

    far = len(bits) - 1
    for i in range(2):
        tsend[i, 0] = owned(i)
        across(i, 0).start()
        join(2 + i)

    def finish_pair(i):
        for at in range(far):
            across(i, at).wait()
            total = tsend[i, at] + trecv[i, at]
            if at + 1 < far:
                tsend[i, at + 1] = total
                across(i, at + 1).start()
        boths[i][side] = total
        pair_copy(boths[i].at[side], boths[i].at[side], b_ss.at[i], b_rs.at[i]).start()

    for i in range(2):
        finish_pair(i)
    for i in (2, 3):
        gwalls[i][dp] = owned(i)
        dp_own(gwalls[i], w_ss.at[i - 2], w_rs.at[i - 2])

    seq_wait(aback, ain, ab_ss, ab_rs)
    adj_in = ain[...].reshape(CHANNELS, STATE).astype(bf16)
    gwrite_ref[0] = (write_intra + dot(tailed, adj_in)).astype(bf16)
    stores[2].start()
    gin_ref[0] = ((gx_intra + tail_w * dot(b, adj_in, NT)) * weight_w).astype(bf16)
    stores[1].start()

    for i in range(2):
        pair_copy(boths[i].at[side], boths[i].at[1 - side], b_ss.at[i], b_rs.at[i]).wait()
        start, size = PIECES[i][1:]
        for d in range(2):
            gw_ref[:, d * wide + start : d * wide + start + size] = boths[i][d]
    for i in (2, 3):
        dp_rest(gwalls[i], w_ss.at[i - 2], w_rs.at[i - 2])
        start, size = PIECES[i][1:]
        for d in range(m):
            at = base + d * cols + start
            gw_ref[:, at : at + size] = gwalls[i][d]
    stores[4].start()

    for i in range(len(PIECES)):
        to_partner(i).wait_send()
    for j in range(halves):
        dp_sent(oall.at[j], o_ss.at[j], o_rs.at[j])
    for i in range(2):
        dp_sent(gwalls[2 + i], w_ss.at[i], w_rs.at[i])
    for store in stores:
        store.wait()


def settle(*refs):
    sources, results, held = refs[:5], refs[5:10], refs[10:15]
    in_sem, out_sem = refs[15:]
    loads = [pltpu.make_async_copy(sources[i], held[i], in_sem.at[i]) for i in range(5)]
    stores = [pltpu.make_async_copy(held[i], results[i], out_sem.at[i]) for i in range(5)]
    for load in loads:
        load.start()
    for load, store in zip(loads, stores):
        load.wait()
        store.start()
    for store in stores:
        store.wait()


def solution(mesh):
    n, m = mesh.shape["seq"], mesh.shape["dp"]

    def shards(inputs, write_vecs, read_vecs, dt_code, a_rate, w_out, grad_out):
        tokens, width = inputs.shape[1], grad_out.shape[2]
        rows, cols = CHANNELS // n, ALONE
        paired_cols = (width - m * ALONE) // 2
        far = m.bit_length() - 2
        hbm = pl.BlockSpec(memory_space=pltpu.MemorySpace.HBM)
        vm = pl.BlockSpec(memory_space=pltpu.VMEM)
        sems = []
        for shape in ((m,), (1,), (n,), (n,), (n,), (n,), (2, m), (4,), (4, n // 2), (2, far), (2,), (2, m)):
            sems += [pltpu.SemaphoreType.DMA(shape)] * 2
        wide, plain = (n, rows + HEADS, STATE), (n, rows, STATE)
        results = (
            jax.ShapeDtypeStruct((1, tokens, CHANNELS), bf16),
            jax.ShapeDtypeStruct((1, tokens, CHANNELS), bf16),
            jax.ShapeDtypeStruct((1, tokens, STATE), bf16),
            jax.ShapeDtypeStruct((1, tokens, STATE), bf16),
            jax.ShapeDtypeStruct((rows, width), f32),
        )
        args = (inputs, write_vecs, read_vecs, dt_code, w_out, grad_out)
        held = pl.pallas_call(
            functools.partial(kernel, n, m, float(tokens * n)),
            out_shape=results,
            in_specs=[hbm] * 4 + [vm] + [hbm] * 2,
            out_specs=(hbm,) * 5,
            scratch_shapes=[pltpu.VMEM(a.shape, a.dtype) for a in args]
            + [pltpu.VMEM(a.shape, a.dtype) for a in results]
            + [
                pltpu.VMEM((m, tokens, cols), f32),
                pltpu.VMEM((m, tokens, cols), f32),
                pltpu.VMEM((tokens, paired_cols), f32),
                pltpu.VMEM((tokens, paired_cols), f32),
                pltpu.VMEM(wide, f32),
                pltpu.VMEM(wide, f32),
                pltpu.VMEM(plain, f32),
                pltpu.VMEM(plain, f32),
                pltpu.VMEM(wide, f32),
                pltpu.VMEM(wide, f32),
                pltpu.VMEM(plain, f32),
                pltpu.VMEM(plain, f32),
                pltpu.VMEM((2, m, tokens, HALF), f32),
            ]
            + [pltpu.VMEM((2, n // 2, rows, size), f32) for _, _, size in PIECES]
            + [pltpu.VMEM((n // 2, rows, size), f32) for _, _, size in PIECES] * 2
            + [pltpu.VMEM((2, far, rows, PIECES[0][2]), f32)] * 2
            + [pltpu.VMEM((2, rows, size), f32) for _, _, size in PIECES[:2]]
            + [pltpu.VMEM((m, rows, size), f32) for _, _, size in PIECES[2:]]
            + sems
            + [pltpu.SemaphoreType.DMA((6,)), pltpu.SemaphoreType.DMA((5,))],
            compiler_params=pltpu.CompilerParams(
                collective_id=0, has_side_effects=True, vmem_limit_bytes=VMEM_BYTES
            ),
            name="scan_core",
        )(inputs, write_vecs, read_vecs, dt_code, a_rate.reshape(1, HEADS), w_out, grad_out)
        return pl.pallas_call(
            settle,
            out_shape=results,
            in_specs=[hbm] * 5,
            out_specs=(hbm,) * 5,
            scratch_shapes=[pltpu.VMEM(a.shape, a.dtype) for a in results]
            + [pltpu.SemaphoreType.DMA((5,)), pltpu.SemaphoreType.DMA((5,))],
            compiler_params=pltpu.CompilerParams(vmem_limit_bytes=VMEM_BYTES),
            name="settle",
        )(*held)

    placed = (
        P("dp", "seq", None),
        P("dp", "seq", None),
        P("dp", "seq", None),
        P("dp", None, "seq"),
        P(),
        P(),
        P("dp", "seq", None),
    )
    return jax.shard_map(
        shards,
        mesh=mesh,
        in_specs=placed,
        out_specs=(
            P("dp", "seq", None),
            P("dp", "seq", None),
            P("dp", "seq", None),
            P("dp", "seq", None),
            P("seq", None),
        ),
        check_vma=False,
    )
```

profile of v0, /device:TPU:13, one launch (start us, length us, event | category | flops | bytes accessed | tf_op | source)
XLA Modules:
  0.0 69.1 jit_solution(15169135228616437195)
XLA Ops:
  0.6 66.2 %scan_core.1 = (bf16[1,256,512]{2,1,0:T(8,128)(2,1)}, bf16[1,256,512]{2,1,0:T(8,128)(2,1)}, bf16[1,256,128]{2,1,0:T(8,128)(2,1)}, bf16[1,256,128]{2,1,0:T(8,128)(2,1)}, f32[64,2560]{1,0:T(8,128)}) custom-call(bf16[1,256,512]{2,1,0:T(8,128)(2,1)} %x_hbm.1, bf16[1,256,128]{2,1,0:T(8,128)(2,1)} %b_hbm.1, bf16[1,256,128]{2,1,0:T(8,128)(2,1)} %c_hbm.1, ...), custom_call_target="tpu_custom_call" | custom-call | tf_op jit(solution)/shard_map/scan_core/pallas_call | solution.py:500
  66.9 2.2 %settle.1 = (bf16[1,256,512]{2,1,0:T(8,128)(2,1)}, bf16[1,256,512]{2,1,0:T(8,128)(2,1)}, bf16[1,256,128]{2,1,0:T(8,128)(2,1)}, bf16[1,256,128]{2,1,0:T(8,128)(2,1)}, f32[64,2560]{1,0:T(8,128)}) custom-call(bf16[1,256,512]{2,1,0:T(8,128)(2,1)} %get-tuple-element.10.refs_0_, bf16[1,256,512]{2,1,0:T(8,128)(2,1)} %get-tuple-element.11.refs_1_, ...), custom_call_target="tpu_custom_call" | custom-call | tf_op jit(solution)/shard_map/settle/pallas_call | solution.py:534
where the time goes:
time: 70.3 us; the launch traced here: 69.1 us
  Pallas kernels  68.5 us (97%)
    pallas_call x1, Pallas kernels, shards(): pl.pallas_call(functools.partial(kernel, n, m, float(tokens * n)), out_sh...  66.2 us
    pallas_call x1, Pallas kernels, shards(): pl.pallas_call(settle, out_shape=results, in_specs=[hbm] * 5, out_specs=(...  2.21 us

commit v1 on v0

--- a/solution.py
+++ b/solution.py
@@ -264,14 +264,8 @@
     loads[5].wait()
     grad_y = dot(grad, w_ref[...], NT).astype(bf16)
     grad_dec = (grad_y.astype(f32) * head_w).astype(bf16)
-    own_adj = dot(grad_dec, c, TN)
-    asend[:, :rows, :] = own_adj.reshape(n, rows, STATE)
-    asend[:, rows:, :] = jnp.broadcast_to(totals[None], (n, HEADS, STATE))
-    seq_start(asend, arecv, a_ss, a_rs)
-
     my_head = (me * rows) // HEAD_DIM
     frecv[me] = fsend[me]
-    arecv[me] = asend[me]
 
     def scan_rows(buf, back, reverse):
         def body(step, state):
@@ -281,11 +275,6 @@
             return decay * state + buf[s, :rows, :]
 
         lax.fori_loop(0, n, body, jnp.zeros((rows, STATE), f32))
-
-    seq_wait(fsend, frecv, f_ss, f_rs)
-    scan_rows(frecv, fback, False)
-    seq_start(fback, fin, fb_ss, fb_rs)
-    fin[me] = fback[me]
 
     scores = dot(c, b, NT)
     y_parts, gx_parts = [], []
@@ -303,10 +292,16 @@
         return pair
 
     pair = within(range(HEADS // 2), jnp.zeros((tokens, tokens), f32))
-    seq_wait(asend, arecv, a_ss, a_rs)
-    scan_rows(arecv, aback, True)
-    seq_start(aback, ain, ab_ss, ab_rs)
-    ain[me] = aback[me]
+    seq_wait(fsend, frecv, f_ss, f_rs)
+    scan_rows(frecv, fback, False)
+    seq_start(fback, fin, fb_ss, fb_rs)
+    fin[me] = fback[me]
+
+    own_adj = dot(grad_dec, c, TN)
+    asend[:, :rows, :] = own_adj.reshape(n, rows, STATE)
+    asend[:, rows:, :] = jnp.broadcast_to(totals[None], (n, HEADS, STATE))
+    seq_start(asend, arecv, a_ss, a_rs)
+    arecv[me] = asend[me]
     pair = within(range(HEADS // 2, HEADS), pair)
     y_intra = jnp.concatenate(y_parts, axis=1)
     gx_intra = jnp.concatenate(gx_parts, axis=1)
@@ -382,6 +377,10 @@
             send_part(i, own_sum + mate_sum)
     gread_ref[0] = (read_intra + dot(grad_dec, state_in)).astype(bf16)
     stores[3].start()
+    seq_wait(asend, arecv, a_ss, a_rs)
+    scan_rows(arecv, aback, True)
+    seq_start(aback, ain, ab_ss, ab_rs)
+    ain[me] = aback[me]
     lax.fori_loop(1, m, g_wait, 0)
     gall_half = [gall[d].astype(bf16) for d in range(m)]
     for i in range(2):

time: 70.3 us -> 66.5 us (0.946)
  Pallas kernels: 68.5 us -> 64.9 us
    pallas_call x1, Pallas kernels: 66.2 us -> 62.6 us  [shards(): pl.pallas_call(functools.partial(kernel, n, m, float(tokens * n)), out_sh...]
where the time goes in v1:
time: 66.5 us; the launch traced here: 65.5 us
  Pallas kernels  64.9 us (98%)
    pallas_call x1, Pallas kernels, shards(): pl.pallas_call(functools.partial(kernel, n, m, float(tokens * n)), out_sh...  62.6 us
    pallas_call x1, Pallas kernels, shards(): pl.pallas_call(settle, out_shape=results, in_specs=[hbm] * 5, out_specs=(...  2.21 us

profile of v1, /device:TPU:13, one launch (start us, length us, event | category | flops | bytes accessed | tf_op | source)
XLA Modules:
  0.0 65.5 jit_solution(11123465113777964798)
XLA Ops:
  0.6 62.6 %scan_core.1 = (bf16[1,256,512]{2,1,0:T(8,128)(2,1)}, bf16[1,256,512]{2,1,0:T(8,128)(2,1)}, bf16[1,256,128]{2,1,0:T(8,128)(2,1)}, bf16[1,256,128]{2,1,0:T(8,128)(2,1)}, f32[64,2560]{1,0:T(8,128)}) custom-call(bf16[1,256,512]{2,1,0:T(8,128)(2,1)} %x_hbm.1, bf16[1,256,128]{2,1,0:T(8,128)(2,1)} %b_hbm.1, bf16[1,256,128]{2,1,0:T(8,128)(2,1)} %c_hbm.1, ...), custom_call_target="tpu_custom_call" | custom-call | tf_op jit(solution)/shard_map/scan_core/pallas_call | solution.py:499
  63.3 2.2 %settle.1 = (bf16[1,256,512]{2,1,0:T(8,128)(2,1)}, bf16[1,256,512]{2,1,0:T(8,128)(2,1)}, bf16[1,256,128]{2,1,0:T(8,128)(2,1)}, bf16[1,256,128]{2,1,0:T(8,128)(2,1)}, f32[64,2560]{1,0:T(8,128)}) custom-call(bf16[1,256,512]{2,1,0:T(8,128)(2,1)} %get-tuple-element.10.refs_0_, bf16[1,256,512]{2,1,0:T(8,128)(2,1)} %get-tuple-element.11.refs_1_, ...), custom_call_target="tpu_custom_call" | custom-call | tf_op jit(solution)/shard_map/settle/pallas_call | solution.py:533

commit v2 on v1

--- a/solution.py
+++ b/solution.py
@@ -261,9 +261,6 @@
     gp_copy.start()
     gall[dp] = gsend[dp]
 
-    loads[5].wait()
-    grad_y = dot(grad, w_ref[...], NT).astype(bf16)
-    grad_dec = (grad_y.astype(f32) * head_w).astype(bf16)
     my_head = (me * rows) // HEAD_DIM
     frecv[me] = fsend[me]
 
@@ -279,36 +276,37 @@
     scores = dot(c, b, NT)
     y_parts, gx_parts = [], []
 
-    def within(heads, pair):
+    masks, mixes = [], []
+    for h in range(HEADS):
+        gap = (cum_col[:, h : h + 1] - cum_row[h : h + 1, :]).astype(f32)
+        mask = jnp.exp(jnp.where(lower, (-rate_row[:, h : h + 1]) * gap, -jnp.inf))
+        mixed = (mask * scores).astype(bf16)
+        masks.append(mask)
+        mixes.append(mixed)
+        y_parts.append(dot(mixed, weighted[:, h * HEAD_DIM : (h + 1) * HEAD_DIM]))
+
+    def backward(heads, pair):
         for h in heads:
             span = slice(h * HEAD_DIM, (h + 1) * HEAD_DIM)
-            gap = (cum_col[:, h : h + 1] - cum_row[h : h + 1, :]).astype(f32)
-            mask = jnp.exp(jnp.where(lower, -(rate_row[:, h : h + 1] * gap), -jnp.inf))
-            mixed = (mask * scores).astype(bf16)
-            w_h, g_h = weighted[:, span], grad_y[:, span]
-            y_parts.append(dot(mixed, w_h))
-            gx_parts.append(dot(mixed, g_h, TN))
-            pair = pair + mask * dot(g_h, w_h, NT)
+            gx_parts.append(dot(mixes[h], grad_y[:, span], TN))
+            pair = pair + masks[h] * dot(grad_y[:, span], weighted[:, span], NT)
         return pair
 
-    pair = within(range(HEADS // 2), jnp.zeros((tokens, tokens), f32))
     seq_wait(fsend, frecv, f_ss, f_rs)
     scan_rows(frecv, fback, False)
     seq_start(fback, fin, fb_ss, fb_rs)
     fin[me] = fback[me]
 
+    loads[5].wait()
+    grad_y = dot(grad, w_ref[...], NT).astype(bf16)
+    grad_dec = (grad_y.astype(f32) * head_w).astype(bf16)
     own_adj = dot(grad_dec, c, TN)
     asend[:, :rows, :] = own_adj.reshape(n, rows, STATE)
     asend[:, rows:, :] = jnp.broadcast_to(totals[None], (n, HEADS, STATE))
     seq_start(asend, arecv, a_ss, a_rs)
     arecv[me] = asend[me]
-    pair = within(range(HEADS // 2, HEADS), pair)
+    pair = backward(range(HEADS // 2), jnp.zeros((tokens, tokens), f32))
     y_intra = jnp.concatenate(y_parts, axis=1)
-    gx_intra = jnp.concatenate(gx_parts, axis=1)
-    pair = pair.astype(bf16)
-    read_intra = dot(pair, b)
-    write_intra = dot(pair, c, TN)
-
     seq_wait(fback, fin, fb_ss, fb_rs)
     state_in = fin[...].reshape(CHANNELS, STATE).astype(bf16)
     out = (y_intra + dot(c, state_in, NT) * head_w).astype(bf16)
@@ -375,12 +373,17 @@
             own_sum = dot(out, gp_own[:, at], TN)
             mate_sum = jnp.concatenate([dot(o, gp_got[:, at], TN) for o in mate_out], axis=0)
             send_part(i, own_sum + mate_sum)
-    gread_ref[0] = (read_intra + dot(grad_dec, state_in)).astype(bf16)
-    stores[3].start()
     seq_wait(asend, arecv, a_ss, a_rs)
     scan_rows(arecv, aback, True)
     seq_start(aback, ain, ab_ss, ab_rs)
     ain[me] = aback[me]
+    pair = backward(range(HEADS // 2, HEADS), pair)
+    gx_intra = jnp.concatenate(gx_parts, axis=1)
+    pair = pair.astype(bf16)
+    read_intra = dot(pair, b)
+    write_intra = dot(pair, c, TN)
+    gread_ref[0] = (read_intra + dot(grad_dec, state_in)).astype(bf16)
+    stores[3].start()
     lax.fori_loop(1, m, g_wait, 0)
     gall_half = [gall[d].astype(bf16) for d in range(m)]
     for i in range(2):
@@ -398,6 +401,13 @@
                 blocks.append(total)
             send_part(i, jnp.concatenate(blocks, axis=0))
 
+    seq_wait(aback, ain, ab_ss, ab_rs)
+    adj_in = ain[...].reshape(CHANNELS, STATE).astype(bf16)
+    gwrite_ref[0] = (write_intra + dot(tailed, adj_in)).astype(bf16)
+    stores[2].start()
+    gin_ref[0] = ((gx_intra + tail_w * dot(b, adj_in, NT)) * weight_w).astype(bf16)
+    stores[1].start()
+
     def across(i, at):
         return pltpu.make_async_remote_copy(
             src_ref=tsend.at[i, at],
@@ -429,13 +439,6 @@
     for i in (2, 3):
         gwalls[i][dp] = owned(i)
         dp_own(gwalls[i], w_ss.at[i - 2], w_rs.at[i - 2])
-
-    seq_wait(aback, ain, ab_ss, ab_rs)
-    adj_in = ain[...].reshape(CHANNELS, STATE).astype(bf16)
-    gwrite_ref[0] = (write_intra + dot(tailed, adj_in)).astype(bf16)
-    stores[2].start()
-    gin_ref[0] = ((gx_intra + tail_w * dot(b, adj_in, NT)) * weight_w).astype(bf16)
-    stores[1].start()
 
     for i in range(2):
         pair_copy(boths[i].at[side], boths[i].at[1 - side], b_ss.at[i], b_rs.at[i]).wait()

time: 66.5 us -> 66.6 us (level)
  no operation moved by 1% of the time
where the time goes in v2:
time: 66.6 us; the launch traced here: 65.4 us
  Pallas kernels  64.8 us (97%)
    pallas_call x1, Pallas kernels, shards(): pl.pallas_call(functools.partial(kernel, n, m, float(tokens * n)), out_sh...  62.6 us
    pallas_call x1, Pallas kernels, shards(): pl.pallas_call(settle, out_shape=results, in_specs=[hbm] * 5, out_specs=(...  2.21 us

profile of v2, /device:TPU:13, one launch (start us, length us, event | category | flops | bytes accessed | tf_op | source)
XLA Modules:
  0.0 65.4 jit_solution(9602513483975966107)
XLA Ops:
  0.6 62.6 %scan_core.1 = (bf16[1,256,512]{2,1,0:T(8,128)(2,1)}, bf16[1,256,512]{2,1,0:T(8,128)(2,1)}, bf16[1,256,128]{2,1,0:T(8,128)(2,1)}, bf16[1,256,128]{2,1,0:T(8,128)(2,1)}, f32[64,2560]{1,0:T(8,128)}) custom-call(bf16[1,256,512]{2,1,0:T(8,128)(2,1)} %x_hbm.1, bf16[1,256,128]{2,1,0:T(8,128)(2,1)} %b_hbm.1, bf16[1,256,128]{2,1,0:T(8,128)(2,1)} %c_hbm.1, ...), custom_call_target="tpu_custom_call" | custom-call | tf_op jit(solution)/shard_map/scan_core/pallas_call | solution.py:502
  63.2 2.2 %settle.1 = (bf16[1,256,512]{2,1,0:T(8,128)(2,1)}, bf16[1,256,512]{2,1,0:T(8,128)(2,1)}, bf16[1,256,128]{2,1,0:T(8,128)(2,1)}, bf16[1,256,128]{2,1,0:T(8,128)(2,1)}, f32[64,2560]{1,0:T(8,128)}) custom-call(bf16[1,256,512]{2,1,0:T(8,128)(2,1)} %get-tuple-element.10.refs_0_, bf16[1,256,512]{2,1,0:T(8,128)(2,1)} %get-tuple-element.11.refs_1_, ...), custom_call_target="tpu_custom_call" | custom-call | tf_op jit(solution)/shard_map/settle/pallas_call | solution.py:536

commit v3 on v2

--- a/solution.py
+++ b/solution.py
@@ -377,6 +377,10 @@
     scan_rows(arecv, aback, True)
     seq_start(aback, ain, ab_ss, ab_rs)
     ain[me] = aback[me]
+    lax.fori_loop(1, m, g_wait, 0)
+    gall_half = [gall[d].astype(bf16) for d in range(m)]
+    join(0)
+    dp_rest(oall.at[0], o_ss.at[0], o_rs.at[0], (1,))
     pair = backward(range(HEADS // 2, HEADS), pair)
     gx_intra = jnp.concatenate(gx_parts, axis=1)
     pair = pair.astype(bf16)
@@ -384,11 +388,8 @@
     write_intra = dot(pair, c, TN)
     gread_ref[0] = (read_intra + dot(grad_dec, state_in)).astype(bf16)
     stores[3].start()
-    lax.fori_loop(1, m, g_wait, 0)
-    gall_half = [gall[d].astype(bf16) for d in range(m)]
-    for i in range(2):
-        join(i)
-        dp_rest(oall.at[i], o_ss.at[i], o_rs.at[i], (1,))
+    join(1)
+    dp_rest(oall.at[1], o_ss.at[1], o_rs.at[1], (1,))
 
     for i, (paired, start, size) in enumerate(PIECES):
         if not paired:

time: 66.6 us -> 66.7 us (level)
  no operation moved by 1% of the time
where the time goes in v3:
time: 66.7 us; the launch traced here: 65.4 us
  Pallas kernels  64.8 us (97%)
    pallas_call x1, Pallas kernels, shards(): pl.pallas_call(functools.partial(kernel, n, m, float(tokens * n)), out_sh...  62.6 us
    pallas_call x1, Pallas kernels, shards(): pl.pallas_call(settle, out_shape=results, in_specs=[hbm] * 5, out_specs=(...  2.21 us

profile of v3, /device:TPU:13, one launch (start us, length us, event | category | flops | bytes accessed | tf_op | source)
XLA Modules:
  0.0 65.4 jit_solution(8711529072496642071)
XLA Ops:
  0.6 62.6 %scan_core.1 = (bf16[1,256,512]{2,1,0:T(8,128)(2,1)}, bf16[1,256,512]{2,1,0:T(8,128)(2,1)}, bf16[1,256,128]{2,1,0:T(8,128)(2,1)}, bf16[1,256,128]{2,1,0:T(8,128)(2,1)}, f32[64,2560]{1,0:T(8,128)}) custom-call(bf16[1,256,512]{2,1,0:T(8,128)(2,1)} %x_hbm.1, bf16[1,256,128]{2,1,0:T(8,128)(2,1)} %b_hbm.1, bf16[1,256,128]{2,1,0:T(8,128)(2,1)} %c_hbm.1, ...), custom_call_target="tpu_custom_call" | custom-call | tf_op jit(solution)/shard_map/scan_core/pallas_call | solution.py:503
  63.2 2.2 %settle.1 = (bf16[1,256,512]{2,1,0:T(8,128)(2,1)}, bf16[1,256,512]{2,1,0:T(8,128)(2,1)}, bf16[1,256,128]{2,1,0:T(8,128)(2,1)}, bf16[1,256,128]{2,1,0:T(8,128)(2,1)}, f32[64,2560]{1,0:T(8,128)}) custom-call(bf16[1,256,512]{2,1,0:T(8,128)(2,1)} %get-tuple-element.10.refs_0_, bf16[1,256,512]{2,1,0:T(8,128)(2,1)} %get-tuple-element.11.refs_1_, ...), custom_call_target="tpu_custom_call" | custom-call | tf_op jit(solution)/shard_map/settle/pallas_call | solution.py:537
